TPU v7x, 32 devices: a whole 2x2x4 slice. The times are simulated.
32 devices in a mesh: seq: 32 (over z, y, x, core).
Axes of the slice: x: 2, y: 2, z: 4, core: 2. Of those that a mesh axis runs over, the one named last changes fastest.
Arguments:
- hidden: bfloat16 [4096, 768], P('seq'), may hold values from -6 to 6
- condition: float32 [6, 768], replicated, may hold values from -6 to 6
- seq_lengths: int32 [6], replicated, may hold values from 1 to 4032, as said below
- w_mod: bfloat16 [768, 2304], replicated, may hold values from -0.21875 to 0.21875
- b_mod: float32 [2304], replicated, may hold values from -2 to 2
- w_in: bfloat16 [768, 3072], replicated, may hold values from -0.21875 to 0.21875
- conv_w: float32 [2, 4, 1536], replicated, may hold values from -3 to 3
- conv_b: float32 [2, 1536], replicated, may hold values from -0.5 to 0.5
- w_x: bfloat16 [2, 1536, 80], replicated, may hold values from -0.15625 to 0.15625
- w_dt: bfloat16 [2, 48, 1536], replicated, may hold values from -0.875 to 0.875
- dt_bias: float32 [2, 1536], replicated, may hold values from -6.5 to -2.3
- a_log: float32 [2, 16, 1536], replicated, may hold values from -9 to 1
- d_skip: float32 [2, 1536], replicated, may hold values from 0.5 to 1.5
- w_out: bfloat16 [1536, 768], replicated, may hold values from -0.4375 to 0.4375
- grad_out: bfloat16 [4096, 768], P('seq'), may hold values from -6 to 6
Outputs:
- output: bfloat16 [4096, 768], P('seq')
- grad_hidden: float32 [4096, 768], P('seq')
- grad_w_mod: float32 [768, 2304], P('seq')
- grad_b_mod: float32 [2304], P('seq')
- grad_w_in: float32 [768, 3072], P('seq')
- grad_conv_w: float32 [2, 4, 1536], P(None, None, 'seq')
- grad_conv_b: float32 [2, 1536], P(None, 'seq')
- grad_w_x: float32 [2, 1536, 80], P(None, 'seq')
- grad_w_dt: float32 [2, 48, 1536], P(None, None, 'seq')
- grad_dt_bias: float32 [2, 1536], P(None, 'seq')
- grad_a_log: float32 [2, 16, 1536], P(None, None, 'seq')
- grad_d_skip: float32 [2, 1536], P(None, 'seq')
- grad_w_out: float32 [1536, 768], P('seq')
Inputs may be any that keep to these rules, and one draw needn't show every extreme that they name: `seq_lengths`: the sequences lie one after another from token 0 and are followed by one or more padding tokens. One of them, which one varies, is a high-resolution image's patch tokens with 4032 tokens; each other one has at most (63) // 5.
All inputs are finite; a program needn't handle non-finite values.
Results may differ from a plain program's by a relative error of at most 0.0097.
Values may be sent and summed in bfloat16 or wider, within the bound.
A program may use at most 192 MiB of HBM per device.

v0:
```python
import functools
import types

import jax
import jax.numpy as jnp
from jax import lax
from jax.experimental import pallas as pl
from jax.experimental.pallas import tpu as pltpu
from jax.sharding import PartitionSpec as P

EPSILON = 1e-06
HIGHEST = lax.Precision.HIGHEST
MESH = pl.DeviceIdType.MESH
LANES = 128
LOG2E = 1.4426950408889634
LN2 = 0.6931471805599453
CUT_STEP = 1e9
PLANE = 8
RIM = 8
CHUNK = 16
XY, YX = (1, 2), (2, 1)
COLS = 256
SCAN = 512
MIB = 1024 * 1024
F32 = jnp.float32
BF16 = jnp.bfloat16
VMEM = pl.BlockSpec(memory_space=pltpu.VMEM)
ANY = pl.BlockSpec(memory_space=pl.ANY)


def shaped(shape, dtype=F32):
    return jax.ShapeDtypeStruct(shape, dtype)


def dot(left, right, dims=((1,), (0,)), precision=None):
    return lax.dot_general(
        left, right, (dims, ((), ())), precision=precision, preferred_element_type=F32
    )


def contract_rows(left, right, precision=None):
    return dot(left, right, ((0,), (0,)), precision)


def contract_cols(left, right):
    return dot(left, right, ((1,), (1,)))


def sigmoid(values):
    return 1.0 / (1.0 + jnp.exp(-values))


def softplus(values):
    return jnp.maximum(values, 0.0) + jnp.log1p(jnp.exp(-jnp.abs(values)))


def tile_at(start):
    return pl.ds(pl.multiple_of(start, LANES), LANES)


def row_of(ref, first, j, lanes):
    eight = pl.ds(pl.multiple_of(first + j // 8 * 8, 8), 8)
    return ref.at[eight, lanes][j % 8 : j % 8 + 1, :]


def segments(positions, bounds):
    total = jnp.full(positions.shape, -1, jnp.int32)
    for bound in bounds:
        total = total + (positions >= bound).astype(jnp.int32)
    return total


def read_bounds(lengths):
    bounds = [jnp.int32(0)]
    for j in range(lengths.shape[0]):
        bounds.append(bounds[-1] + lengths[j])
    return bounds


def rows_iota(rows):
    return lax.broadcasted_iota(jnp.int32, (rows, LANES), 0)


def offset_of(d, k, taps):
    return k - (taps - 1) if d == 0 else taps - 1 - k


def slot_of(o, count, order):
    bits = [o & 1, o >> 1 & 1, o >> 2 & 1]
    return bits[0], (bits[order[0]] * 2 + bits[order[1]]) * (count // PLANE) + o // PLANE


def slot_rows(count, inner):
    rows = inner // count
    return rows + -rows % 16


def stacked_rows(source, stage, o, rows, begin, end):
    middle = (begin + end) // 2
    part = pl.ds(o * rows, rows)
    if rows % 8 == 0:
        return jnp.concatenate([source[part, begin:middle], source[part, middle:end]], axis=0)
    stage[0:rows, :] = source[part, begin:middle]
    stage[rows : 2 * rows, :] = source[part, middle:end]
    return stage[...]


class Refs:
    def __init__(self, names, refs):
        for name, ref in zip(names, refs):
            setattr(self, name, ref)


def token_masks(r, first):
    tokens = r.hidden.shape[0]
    wide = r.normed.shape[0]
    taps = r.conv_w.shape[1]
    bounds = read_bounds(r.lengths)
    position = first + rows_iota(tokens)
    segment = segments(position, bounds)
    for offset in range(1 - taps, taps):
        r.masks[offset + taps - 1] = (segments(position + offset, bounds) == segment).astype(F32)
    wide_segment = segments(first - RIM + rows_iota(wide), bounds)
    lane = lax.broadcasted_iota(jnp.int32, (wide, LANES), 1)
    r.hot[...] = (wide_segment == lane).astype(F32)
    return segment, wide_segment


def normalise(r, below, above):
    tokens = r.hidden.shape[0]
    x = jnp.concatenate([below, r.hidden[...].astype(F32), above], axis=0)
    centered = x - jnp.mean(x, axis=1, keepdims=True)
    scaling = lax.rsqrt(jnp.mean(centered * centered, axis=1, keepdims=True) + EPSILON)
    r.normed[...] = centered * scaling
    r.rescale[...] = jnp.broadcast_to(scaling[RIM : RIM + tokens], (tokens, LANES))


def modulate(r, segment, wide_segment):
    tokens, model = r.hidden.shape
    seqs = r.condition.shape[0]
    for c in range(model // LANES):
        lanes = slice(c * LANES, (c + 1) * LANES)

        def rows_for(part, segs):
            total = jnp.zeros(segs.shape, F32)
            at = part * model + c * LANES
            bias = r.b_mod[at // LANES : at // LANES + 1, :]
            for j in range(seqs):
                row = r.modulation[j : j + 1, at : at + LANES] + bias
                total = jnp.where(segs == j, row, total)
            return total

        one_scale = 1.0 + rows_for(1, wide_segment)
        mixed_in = r.normed[:, lanes] * one_scale + rows_for(0, wide_segment)
        r.mixer[:, lanes] = mixed_in.astype(BF16)
        r.mixer_own[:, lanes] = mixed_in[RIM : RIM + tokens].astype(BF16)
        r.scale1[:, lanes] = one_scale[RIM : RIM + tokens]
        gate = rows_for(2, segment)
        r.gate_rows[:, lanes] = gate
        r.branch_grad[:, lanes] = (r.grad_out[:, lanes].astype(F32) * gate).astype(BF16)


def project(r):
    tokens, inner = r.seed.shape
    r.proj[...] = jnp.zeros_like(r.proj)

    def block(b, none):
        cols = pl.ds(pl.multiple_of(b * COLS, COLS), COLS)
        conv = dot(r.mixer[...], r.w_conv[:, cols]).astype(BF16)
        r.conv_keep[:, cols] = conv
        r.conv_wide[...] = conv.astype(F32)
        gate = dot(r.mixer_own[...], r.w_gate[:, cols])
        r.gate_branch[:, cols] = gate
        back = contract_cols(r.branch_grad[...], r.w_out[cols, :])
        r.gated_grad[:, cols] = back
        r.seed[:, cols] = back * (gate * sigmoid(gate))
        convolve(r, 0, b)
        return none

    lax.fori_loop(0, inner // COLS, block, 0)


def convolve(r, d, b):
    tokens, inner = r.seed.shape
    taps = r.conv_w.shape[1]
    cols = pl.ds(pl.multiple_of(b * COLS, COLS), COLS)
    acts = []
    for c in range(COLS // LANES):
        lanes = tile_at(b * COLS + c * LANES)
        here = slice(c * LANES, (c + 1) * LANES)
        total = jnp.broadcast_to(r.conv_b[d : d + 1, lanes], (tokens, LANES))
        for k in range(taps):
            offset = offset_of(d, k, taps)
            total = total + r.conv_w[d, k : k + 1, lanes] * (
                r.conv_wide[RIM + offset : RIM + offset + tokens, here]
                * r.masks[offset + taps - 1]
            )
        sigma = sigmoid(total)
        r.conv_slope[d, :, lanes] = (sigma * (1.0 + total * (1.0 - sigma))).astype(BF16)
        act = (total * sigma).astype(BF16)
        r.active[d, :, lanes] = act
        acts.append(act)
    r.proj[d] += contract_cols(jnp.concatenate(acts, axis=1), r.w_x[d, :, cols])


def convolve_reverse(r):
    inner = r.seed.shape[1]

    def block(b, none):
        cols = pl.ds(pl.multiple_of(b * COLS, COLS), COLS)
        r.conv_wide[...] = r.conv_keep[:, cols].astype(F32)
        convolve(r, 1, b)
        return none

    lax.fori_loop(0, inner // COLS, block, 0)


def coefficients(r, d):
    tokens = r.seed.shape[0]
    rank = r.w_dt.shape[1]
    states = r.rate.shape[1]
    place = lax.rem(lax.broadcasted_iota(jnp.int32, (tokens, CHUNK * states), 0), CHUNK)
    owner = lax.broadcasted_iota(jnp.int32, (tokens, CHUNK * states), 1) // states
    on_diag = place == owner
    column = lax.rem(lax.broadcasted_iota(jnp.int32, (states, CHUNK * states), 1), states)
    repeat = (column == lax.broadcasted_iota(jnp.int32, (states, CHUNK * states), 0)).astype(BF16)
    whole = r.proj[d]
    r.rank_low[d] = whole[:, :rank].astype(BF16)
    flipped = whole.T
    for start, blk, spread in (
        (rank, r.in_blk, r.in_spread),
        (rank + states, r.out_blk, r.out_spread),
    ):
        coef = whole[:, start : start + states].astype(BF16)
        blk[d] = jnp.where(on_diag, dot(coef, repeat), 0.0).astype(BF16)
        rows = flipped[start : start + states, :]
        for t in range(tokens):
            spread[d, t * states : (t + 1) * states, :] = jnp.broadcast_to(
                rows[:, t : t + 1], (states, LANES)
            )


def step_logits(r, d, cols):
    return dot(r.rank_low[d], r.w_dt[d, :, cols]) + r.dt_bias[d : d + 1, cols]


def stepping(r, d):
    inner = r.seed.shape[1]
    taps = r.conv_w.shape[1]

    def block(b, none):
        cols = pl.ds(pl.multiple_of(b * COLS, COLS), COLS)
        step = softplus(step_logits(r, d, cols))
        keep = r.masks[taps - 2] if d == 0 else r.masks[taps]
        keep = jnp.concatenate([keep] * (COLS // LANES), axis=1)
        r.masked[d, :, cols] = jnp.where(keep > 0.5, step, CUT_STEP)
        r.driven[d, :, cols] = step * r.active[d, :, cols].astype(F32)
        return none

    lax.fori_loop(0, inner // COLS, block, 0)


def state_rows(ref, d, first, j, states):
    return ref[d, pl.ds(pl.multiple_of((first + j) * states, states), states), :]


def summarise(r, d, begin, end):
    tokens, inner = r.seed.shape
    states = r.rate.shape[1]
    tiles = inner // LANES
    per = SCAN // LANES

    def block(b, none):
        lanes = [tile_at(b * SCAN + c * LANES) for c in range(per)]

        def group(i, carry):
            carry = list(carry)
            start = pl.multiple_of((i if d == 0 else tokens // 8 - 1 - i) * 8, 8)
            for k in range(8):
                j = k if d == 0 else 7 - k
                in_row = state_rows(r.in_spread, d, start, j, states)
                out_row = state_rows(r.out_spread, d, start, j, states)
                for c in range(per):
                    state, decay, adj = carry[c]
                    now = jnp.exp2(
                        row_of(r.masked.at[d], start, j, lanes[c]) * r.rate[d, :, lanes[c]]
                    )
                    state = now * state + in_row * row_of(r.driven.at[d], start, j, lanes[c])
                    decay = decay * now
                    adj = adj + decay * (out_row * row_of(r.seed, start, j, lanes[c]))
                    carry[c] = (state, decay, adj)
            return tuple(carry)

        zero = jnp.zeros((states, LANES), F32)
        one = jnp.ones((states, LANES), F32)
        carry = lax.fori_loop(0, tokens // 8, group, tuple((zero, one, zero) for _ in range(per)))
        for c in range(per):
            state, decay, adj = carry[c]
            down, up = (adj, state) if d == 0 else (state, adj)
            at = d * tiles + b * per + c
            r.sums[at, 0] = down.astype(BF16)
            r.sums[at, 1] = three_pieces(
                jnp.sum(r.masked[d, :, lanes[c]], axis=0, keepdims=True), states
            )
            r.sums[at, 2] = up.astype(BF16)
        return none

    lax.fori_loop(begin, end, block, 0)


def three_pieces(row, states):
    high = row.astype(BF16).astype(F32)
    middle = (row - high).astype(BF16).astype(F32)
    lowest = row - high - middle
    at = lax.broadcasted_iota(jnp.int32, (states, row.shape[-1]), 0)
    return jnp.where(
        at == 0, high, jnp.where(at == 1, middle, jnp.where(at == 2, lowest, 0.0))
    ).astype(BF16)


def remote(src, dst, sems, slot, peer, there=None):
    return pltpu.make_async_remote_copy(
        src_ref=src,
        dst_ref=dst,
        send_sem=sems[0].at[slot],
        recv_sem=sems[1].at[slot if there is None else there],
        device_id=(peer,),
        device_id_type=MESH,
    )


class Place:
    def __init__(self, count):
        self.count = count
        self.groups = count // PLANE
        self.me = lax.axis_index("seq")
        self.bits = [lax.rem(self.me, 2), lax.rem(self.me // 2, 2), lax.rem(self.me // 4, 2)]
        self.flips = [self.me + (1 - 2 * self.bits[i]) * (1 << i) for i in range(3)]
        self.level = self.me // PLANE
        self.low = lax.rem(self.me, PLANE)
        self.left = lax.rem(self.me + count - 1, count)
        self.right = lax.rem(self.me + 1, count)
        self.far = [lax.rem(self.level + k, self.groups) for k in range(1, self.groups)]

    def peers(self):
        base = self.level * PLANE
        peers = [base + lax.rem(self.low + k, PLANE) for k in range(1, PLANE)]
        return peers + [self.left, self.right] + [g * PLANE + self.low for g in self.far]


def add_into(into, own, first):
    def one(i, none):
        into[i] = into[i] + own[first + i]
        return none

    lax.fori_loop(0, into.shape[0], one, 0)


class Carries:
    def __init__(self, r, place, sems):
        self.r, self.place, self.sems = r, place, sems
        self.mine = place.low
        self.base = place.level * PLANE
        self.share = r.sums.shape[0] // PLANE

    def rows(self, j):
        return pl.ds(j * self.share, self.share)

    def combiners(self, d):
        return range(d * PLANE // 2, (d + 1) * PLANE // 2)

    def combines(self, d):
        return self.mine // (PLANE // 2) == d

    def out(self, j):
        r = self.r
        src, dst = r.sums.at[self.rows(j)], r.got.at[self.mine]
        return remote(src, dst, self.sems[0], j, self.base + j, self.mine)

    def arrival(self, s):
        r = self.r
        return remote(r.sums.at[self.rows(s)], r.got.at[s], self.sems[0], s, self.base + s)

    def back(self, j):
        r = self.r
        src, dst = r.back.at[j], r.entering.at[self.rows(self.mine)]
        return remote(src, dst, self.sems[2], j, self.base + j, self.mine)

    def entry(self, s):
        r = self.r
        return remote(
            r.back.at[s], r.entering.at[self.rows(s)], self.sems[2], s, self.base + s
        )

    def between(self):
        r, place = self.r, self.place
        copies = []
        for k, other in enumerate(place.far):
            start = jnp.where(other > place.level, 1, 0)
            src, dst = r.total.at[pl.ds(start, 2)], r.others.at[place.level]
            copies.append(remote(src, dst, self.sems[1], k, other * PLANE + self.mine))
        return copies

    def send(self, d):
        for j in self.combiners(d):

            @pl.when(self.mine != j)
            def _():
                self.out(j).start()

    def whole(self, pieces):
        pieces = pieces.astype(F32)
        return pieces[:, 0:1] + pieces[:, 1:2] + pieces[:, 2:3]

    def rates(self):
        r = self.r
        tiles = r.rate.shape[2] // LANES
        parts = []
        for c in range(self.share):
            at = self.mine * self.share + c
            parts.append(r.rate[at // tiles, :, tile_at(lax.rem(at, tiles) * LANES)][None])
        return jnp.concatenate(parts, axis=0)

    def combine(self, d):
        r = self.r

        @pl.when(self.combines(d))
        def _():
            mine, share = self.mine, self.share
            states = r.rate.shape[1]
            r.got[mine] = r.sums[self.rows(mine)]
            r.others[self.place.level] = jnp.zeros(r.others.shape[1:], BF16)
            for s in range(PLANE):

                @pl.when(mine != s)
                def _():
                    self.arrival(s).wait_recv()

            rates = self.rates()
            block = (share, states, LANES)
            up = jnp.zeros(block, F32)
            down = jnp.zeros(block, F32)
            time = jnp.zeros((share, 1, LANES), F32)
            for j in range(PLANE):
                now = self.whole(r.got[j, :, 1])
                up = jnp.exp2(rates * now) * up + r.got[j, :, 2].astype(F32)
                time = time + now
            for j in reversed(range(PLANE)):
                now = jnp.exp2(rates * self.whole(r.got[j, :, 1]))
                down = now * down + r.got[j, :, 0].astype(F32)
            r.total[0] = down.astype(BF16)
            for c in range(share):
                r.total[1, c] = three_pieces(time[c], states)
            r.total[2] = up.astype(BF16)
            for copy in self.between():
                copy.start()

    def spread(self, d):
        r = self.r

        @pl.when(self.combines(d))
        def _():
            mine, share, level = self.mine, self.share, self.place.level
            states = r.rate.shape[1]
            groups = self.place.groups
            for copy in self.between():
                copy.wait_recv()
            rates = self.rates()
            block = (share, states, LANES)
            up = jnp.zeros(block, F32)
            for g in range(groups):
                decay = jnp.exp2(rates * self.whole(r.others[g, 0]))
                up = jnp.where(g < level, decay * up + r.others[g, 1].astype(F32), up)
            down = jnp.zeros(block, F32)
            for g in reversed(range(groups)):
                decay = jnp.exp2(rates * self.whole(r.others[g, 1]))
                down = jnp.where(g > level, decay * down + r.others[g, 0].astype(F32), down)
            decays = [jnp.exp2(rates * self.whole(r.got[j, :, 1])) for j in range(PLANE)]
            for j in range(PLANE):
                r.back[j, :, 0] = up.astype(BF16)
                up = decays[j] * up + r.got[j, :, 2].astype(F32)
            for j in reversed(range(PLANE)):
                r.back[j, :, 1] = down.astype(BF16)
                down = decays[j] * down + r.got[j, :, 0].astype(F32)
            for j in range(PLANE):

                @pl.when(mine != j)
                def _():
                    self.back(j).start()

            r.entering[self.rows(mine)] = r.back[mine]

    def receive(self, d):
        for s in self.combiners(d):

            @pl.when(self.mine != s)
            def _():
                self.entry(s).wait_recv()

    def finish(self):
        for j in range(PLANE):

            @pl.when(self.mine != j)
            def _():
                self.out(j).wait_send()
                self.back(j).wait_send()

        for copy in self.between():
            copy.wait_send()


class Piece:
    def __init__(self, place, order, part, own, refs):
        self.place, self.order, self.part, self.own = place, order, part, own
        self.got1, self.got2, self.got3, self.got4 = refs[:4]
        self.sems = refs[4:]
        self.bits = [place.bits[0], place.bits[order[0]], place.bits[order[1]]]
        self.flips = [place.flips[0], place.flips[order[0]], place.flips[order[1]]]

    def hop(self, i):
        if i == 0:
            src = self.part.at[1 - self.bits[0]]
        else:
            half = 4 * self.place.groups >> i
            held = (self.got1, self.got2)[i - 1]
            src = held.at[pl.ds((1 - self.bits[i]) * half, half)]
        return remote(src, (self.got1, self.got2, self.got3)[i], self.sems, i, self.flips[i])

    def fan(self):
        return [
            remote(
                self.got3.at[g],
                self.got4.at[self.place.level],
                self.sems,
                3 + k,
                g * PLANE + self.place.low,
            )
            for k, g in enumerate(self.place.far)
        ]

    def step(self, i):
        groups = self.place.groups
        if i:
            self.hop(i - 1).wait_recv()
        if i == 1:
            add_into(self.got1, self.own, 0)
        elif i == 2:
            add_into(self.got2, self.got1, self.bits[1] * 2 * groups)
        elif i == 3:
            add_into(self.got3, self.got2, self.bits[2] * groups)
        if i < 3:
            self.hop(i).start()
            return
        for copy in self.fan():
            copy.start()
        self.got4[self.place.level] = self.got3[self.place.level]

    def end(self, share, begin):
        for copy in self.fan():
            copy.wait_recv()
        total = self.got4[0].astype(F32)
        for g in range(1, self.place.groups):
            total = total + self.got4[g].astype(F32)
        share[:, begin : begin + total.shape[1]] = total
        for copy in [self.hop(1), self.hop(2)] + self.fan():
            copy.wait_send()

    def release(self):
        self.hop(0).wait_send()


def piece_scratch(rows, cols, groups):
    return [
        pltpu.VMEM((size, rows, cols), BF16) for size in (4 * groups, 2 * groups, groups, groups)
    ] + [pltpu.SemaphoreType.DMA((2 + groups,))] * 2


def interleaved(chunks, compute, pieces, carry):
    jobs = []
    for i in range(chunks):
        carry = compute(i, i % 2, carry, jobs)
        jobs = pieces(i, i % 2)
    for job in jobs:
        job()
    return carry


def jobs_between(jobs, k):
    every = max(CHUNK // max(len(jobs), 1), 1)
    if jobs and k % every == 0 and k // every < len(jobs):
        jobs[k // every]()


def small_rows(taps):
    return 0, 2 * taps, 2 * taps + 2, 2 * taps + 4, 2 * taps + 8


def forward_scan(r, d):
    tokens, inner = r.seed.shape
    tiles = inner // LANES
    per = SCAN // LANES
    states = r.rate.shape[1]
    chunks = tokens // CHUNK
    rows = (r.rows0, r.rows1)

    def first_of(i):
        return (i if d == 0 else chunks - 1 - i) * CHUNK

    def block(b, none):
        cols = pl.ds(pl.multiple_of(b * SCAN, SCAN), SCAN)
        lanes = [tile_at(b * SCAN + c * LANES) for c in range(per)]
        edge = d * tokens * states
        for c in range(per):
            r.kept[edge : edge + states, lanes[c]] = r.entering[d * tiles + b * per + c, d]

        def compute(i, side, carry, jobs):
            carry = list(carry)
            first = first_of(i)
            for k in range(CHUNK):
                jobs_between(jobs, k)
                j = k if d == 0 else CHUNK - 1 - k
                in_row = state_rows(r.in_spread, d, first, j, states)
                for c in range(per):
                    now = jnp.exp2(
                        row_of(r.masked.at[d], first, j, lanes[c]) * r.rate[d, :, lanes[c]]
                    )
                    state = now * carry[c] + in_row * row_of(r.driven.at[d], first, j, lanes[c])
                    rows[side][
                        j * states : (j + 1) * states, c * LANES : (c + 1) * LANES
                    ] = state.astype(BF16)
                    carry[c] = state
            return tuple(carry)

        def pieces(i, side):
            here = pl.ds(first_of(i), CHUNK)

            def keep(q):
                half = CHUNK * states // 2
                slot = (first_of(i) + 1 - d) * states + q * half
                r.kept[slot : slot + half, cols] = rows[side][q * half : (q + 1) * half, :]

            def mix(q):
                part = pl.ds(pl.multiple_of(b * SCAN + q * COLS, COLS), COLS)
                mixed = dot(r.out_blk[d, here, :], rows[side][:, q * COLS : (q + 1) * COLS])
                if d == 0:
                    r.mixed[here, part] = mixed
                else:
                    r.mixed[here, part] += mixed

            def grad():
                r.out_acc[d, here, :] += contract_cols(
                    r.seed[here, cols].astype(BF16), rows[side][...]
                )

            return [
                functools.partial(mix, 0),
                functools.partial(keep, 0),
                functools.partial(mix, 1),
                functools.partial(keep, 1),
                grad,
            ]

        start = tuple(r.entering[d * tiles + b * per + c, d].astype(F32) for c in range(per))
        interleaved(chunks, compute, pieces, start)
        return none

    lax.fori_loop(0, inner // SCAN, block, 0)


def adjoint_scan(r, d, begin, end):
    tokens, inner = r.seed.shape
    tiles = inner // LANES
    per = SCAN // LANES
    states = r.rate.shape[1]
    taps = r.conv_w.shape[1]
    chunks = tokens // CHUNK
    wide = CHUNK * states
    adjs = (r.rows0, r.rows1)
    slopes = (r.slope0, r.slope1)
    ones = (
        lax.broadcasted_iota(jnp.int32, (CHUNK, wide), 1) // states
        == lax.broadcasted_iota(jnp.int32, (CHUNK, wide), 0)
    ).astype(BF16)

    def first_of(i):
        return (chunks - 1 - i if d == 0 else i) * CHUNK

    def block(b, none):
        cols = pl.ds(pl.multiple_of(b * SCAN, SCAN), SCAN)
        lanes = [tile_at(b * SCAN + c * LANES) for c in range(per)]
        low_rates = [r.rate[d, :, lanes[c]].astype(BF16) for c in range(per)]

        def compute(i, side, carry, jobs):
            carry = list(carry)
            first = first_of(i)
            for k in range(CHUNK):
                jobs_between(jobs, k)
                j = CHUNK - 1 - k if d == 0 else k
                slot = (first + j + d) * states
                out_row = state_rows(r.out_spread, d, first, j, states)
                part = slice(j * states, (j + 1) * states)
                for c in range(per):
                    here = slice(c * LANES, (c + 1) * LANES)
                    coming, total = carry[c]
                    step = row_of(r.masked.at[d], first, j, lanes[c])
                    now = jnp.exp2(step * r.rate[d, :, lanes[c]])
                    adj = out_row * row_of(r.seed, first, j, lanes[c]) + coming
                    coming = now * adj
                    slope = coming.astype(BF16) * r.kept[slot : slot + states, lanes[c]]
                    slope = slope * low_rates[c]
                    total = total + slope.astype(F32) * step
                    adjs[side][part, here] = adj.astype(BF16)
                    slopes[side][part, here] = slope
                    carry[c] = (coming, total)
            return tuple(carry)

        def pieces(i, side):
            here = pl.ds(first_of(i), CHUNK)

            def driven_side(q):
                part = pl.ds(pl.multiple_of(b * SCAN + q * COLS, COLS), COLS)
                r.driven_grad[d][here, part] = dot(
                    r.in_blk[d, here, :], adjs[side][:, q * COLS : (q + 1) * COLS]
                )

            def decay_side(q):
                part = pl.ds(pl.multiple_of(b * SCAN + q * COLS, COLS), COLS)
                r.decay_grad[d][here, part] = (
                    dot(ones, slopes[side][:, q * COLS : (q + 1) * COLS]) * LN2
                )

            def in_side():
                r.in_acc[d, here, :] += contract_cols(
                    r.driven[d, here, cols].astype(BF16), adjs[side][...]
                )

            return [
                functools.partial(driven_side, 0),
                functools.partial(decay_side, 0),
                in_side,
                functools.partial(driven_side, 1),
                functools.partial(decay_side, 1),
            ]

        zero = jnp.zeros((states, LANES), F32)
        start = tuple(
            (r.entering[d * tiles + b * per + c, 1 - d].astype(F32), zero) for c in range(per)
        )
        carry = interleaved(chunks, compute, pieces, start)
        at_rate = small_rows(taps)[4]
        for c in range(per):
            r.small[at_rate + d * states : at_rate + (d + 1) * states, lanes[c]] = (
                carry[c][1] * LN2
            )
        return none

    lax.fori_loop(begin, end, block, 0)


def output_half(r, count, half):
    tokens, inner = r.mixed.shape
    model = r.hidden.shape[1]
    begin = half * inner // COLS // 2

    def block(b, none):
        cols = pl.ds(pl.multiple_of(b * COLS, COLS), COLS)
        mixed = r.mixed[:, cols]
        for d in range(2):
            mixed = mixed + r.d_skip[d : d + 1, cols] * r.active[d, :, cols].astype(F32)
        gate = r.gate_branch[:, cols]
        sigma = sigmoid(gate)
        now = (mixed * (gate * sigma)).astype(BF16)
        r.gated[:, cols] = now
        slope = sigma * (1.0 + gate * (1.0 - sigma))
        back = (r.gated_grad[:, cols] * mixed * slope).astype(BF16)
        r.gate_branch_grad[:, cols] = back
        r.branch[...] += dot(now, r.w_out[cols, :])
        here = pl.ds(pl.multiple_of((b - begin) * COLS, COLS), COLS)
        r.whole[:, here] = contract_rows(r.mixer_own[...], back)
        return none

    lax.fori_loop(begin, begin + inner // COLS // 2, block, 0)
    part = (r.gate0, r.gate1)[half]
    for o in range(count):
        first, later = slot_of(o, count, (XY, YX)[half])
        part[first, later] = stacked_rows(
            r.whole, r.stage, o, model // count, 0, model
        ).astype(BF16)


def output_weights(r, count):
    tokens, inner = r.mixed.shape
    model = r.hidden.shape[1]
    rows = inner // count
    half = model // 2
    chunk = inner // 8
    per = count // 8
    for q in range(8):
        r.whole[0:chunk, :] = contract_rows(
            r.gated[:, q * chunk : (q + 1) * chunk], r.branch_grad[...]
        )
        for i in range(per):
            low = r.whole[i * rows : (i + 1) * rows, :].astype(BF16)
            first, later = slot_of(q * per + i, count, XY)
            r.out0[first, later, 0:rows] = low[:, :half]
            first, later = slot_of(q * per + i, count, YX)
            r.out1[first, later, 0:rows] = low[:, half:]


def column_sum(values):
    return jnp.sum(values, axis=0, keepdims=True)


def through_steps(r):
    tokens, inner = r.seed.shape
    taps = r.conv_w.shape[1]
    rank = r.w_dt.shape[1]
    proj = r.w_x.shape[1]
    states = r.rate.shape[1]
    _, _, at_dt, at_skip, _ = small_rows(taps)
    r.rank_grad[...] = jnp.zeros_like(r.rank_grad)

    def block(b, none):
        cols = pl.ds(pl.multiple_of(b * COLS, COLS), COLS)
        for d in range(2):
            act = r.active[d, :, cols].astype(F32)
            value = step_logits(r, d, cols)
            back = r.driven_grad[d][:, cols]
            grown = r.seed[:, cols]
            grad = (r.decay_grad[d][:, cols] + back * act) * sigmoid(value)
            low = grad.astype(BF16)
            r.driven_grad[d][:, cols] = (
                back * softplus(value) + grown * r.d_skip[d : d + 1, cols]
            )
            r.small[at_dt + d : at_dt + d + 1, cols] = column_sum(grad)
            r.small[at_skip + d : at_skip + d + 1, cols] = column_sum(grown * act)
            r.rank_grad[d] += contract_cols(low, r.w_dt[d, :, cols])
            r.in_spread[d, cols, proj : proj + rank] = contract_rows(low, r.rank_low[d])
        return none

    lax.fori_loop(0, inner // COLS, block, 0)

    place = lax.rem(lax.broadcasted_iota(jnp.int32, (tokens, CHUNK * states), 0), CHUNK)
    owner = lax.broadcasted_iota(jnp.int32, (tokens, CHUNK * states), 1) // states
    on_diag = place == owner
    column = lax.rem(lax.broadcasted_iota(jnp.int32, (CHUNK * states, states), 0), states)
    gather = (column == lax.broadcasted_iota(jnp.int32, (CHUNK * states, states), 1)).astype(BF16)
    for d in range(2):
        r.proj_grad[d, :, 0:rank] = r.rank_grad[d].astype(BF16)
        for start, acc in ((rank, r.in_acc), (rank + states, r.out_acc)):
            kept = jnp.where(on_diag, acc[d], 0.0).astype(BF16)
            r.proj_grad[d, :, start : start + states] = dot(kept, gather).astype(BF16)

    def weights(b, none):
        cols = pl.ds(pl.multiple_of(b * COLS, COLS), COLS)
        for d in range(2):
            r.in_spread[d, cols, 0:proj] = contract_rows(r.active[d, :, cols], r.proj_grad[d])
        return none

    lax.fori_loop(0, inner // COLS, weights, 0)


def through_conv(r, begin, end):
    tokens, inner = r.seed.shape
    taps = r.conv_w.shape[1]
    at_conv, at_bias, _, _, _ = small_rows(taps)

    def block(b, none):
        cols = pl.ds(pl.multiple_of(b * COLS, COLS), COLS)
        r.conv_wide[...] = r.conv_keep[:, cols].astype(F32)
        r.input_wide[...] = jnp.zeros_like(r.input_wide)
        for d in range(2):
            total = r.driven_grad[d][:, cols] + dot(r.proj_grad[d], r.w_x[d, :, cols])
            for c in range(COLS // LANES):
                lanes = tile_at(b * COLS + c * LANES)
                here = slice(c * LANES, (c + 1) * LANES)
                grad = total[:, here] * r.conv_slope[d, :, lanes].astype(F32)
                r.small[at_bias + d : at_bias + d + 1, lanes] = column_sum(grad)
                for k in range(taps):
                    offset = offset_of(d, k, taps)
                    window = slice(RIM + offset, RIM + offset + tokens)
                    part = grad * r.masks[offset + taps - 1]
                    at = at_conv + d * taps + k
                    r.small[at : at + 1, lanes] = column_sum(part * r.conv_wide[window, here])
                    r.input_wide[window, here] += r.conv_w[d, k : k + 1, lanes] * part
        low = r.input_wide[...].astype(BF16)
        here = pl.ds(pl.multiple_of((b - begin) * COLS, COLS), COLS)
        r.whole[:, here] = contract_rows(r.mixer[...], low)
        r.norm_wide[...] += contract_cols(low, r.w_conv[:, cols])
        r.norm_wide[RIM : RIM + tokens, :] += contract_cols(
            r.gate_branch_grad[:, cols], r.w_gate[:, cols]
        )
        r.small_cols[cols, :] = r.small[:, cols].T
        return none

    lax.fori_loop(begin, end, block, 0)


def fill_columns(r, part, count):
    rows = r.seed.shape[1] // count
    for o in range(count):
        first, later = slot_of(o, count, XY)
        for d in range(2):
            part[first, later, 0:rows, d * LANES : (d + 1) * LANES] = r.in_spread[
                d, o * rows : (o + 1) * rows, :
            ].astype(BF16)


def fill_conv(r, parts, count):
    inner = r.seed.shape[1]
    model = r.normed.shape[1]
    rows, mrows = inner // count, model // count
    for o in range(count):
        both = stacked_rows(r.whole, r.stage, o, mrows, 0, model).astype(BF16)
        if len(parts) == 1:
            first, later = slot_of(o, count, YX)
            parts[0][first, later] = both
            continue
        cut = parts[0].shape[3]
        rest = model // 2 - cut
        first, later = slot_of(o, count, XY)
        parts[0][first, later] = both[:, :cut]
        first, later = slot_of(o, count, YX)
        parts[1][first, later, :, 0:rest] = both[:, cut:]
        parts[1][first, later, 0:rows, rest:] = r.small_cols[o * rows : (o + 1) * rows, :].astype(
            BF16
        )


def modulation_shares(r, place):
    seqs, model = r.condition.shape
    mrows = r.w_mod_share.shape[0]
    width = r.b_mod_share.shape[1]

    def picked(total, number):
        source = lax.broadcasted_iota(jnp.int32, (total, number), 0)
        return source == place.me * number + lax.broadcasted_iota(jnp.int32, (total, number), 1)

    cond = r.condition[...]
    cond_act = (cond * sigmoid(cond)).astype(BF16)
    my_cond = dot(cond_act, picked(model, mrows).astype(BF16))
    totals = r.mod[0:seqs, :]
    r.w_mod_share[...] = contract_rows(my_cond, totals, HIGHEST)
    bias = jnp.broadcast_to(jnp.sum(totals, axis=0, keepdims=True), (8, 3 * model))
    r.b_mod_share[...] = dot(bias, picked(3 * model, width).astype(F32), precision=HIGHEST)[0:1]


def input_gradient(r, place):
    tokens, model = r.hidden.shape
    norm_grad = r.norm_wide[RIM : RIM + tokens, :]
    low = jnp.where(place.me > 0, r.edge_got[0:RIM, :], 0.0)
    high = jnp.where(place.me < place.count - 1, r.edge_got[RIM:, :], 0.0)
    middle = jnp.zeros((tokens - 2 * RIM, model), F32)
    norm_grad = norm_grad + jnp.concatenate([low, middle, high], axis=0)
    scaled = norm_grad * r.scale1[...]
    normal = r.normed[RIM : RIM + tokens, :]
    r.grad_x[...] = r.grad_out[...].astype(F32) + r.rescale[:, 0:1] * (
        scaled
        - jnp.mean(scaled, axis=1, keepdims=True)
        - normal * jnp.mean(scaled * normal, axis=1, keepdims=True)
    )


def modulation_sums(r):
    tokens = r.seed.shape[0]
    model = r.normed.shape[1]
    seqs = r.mod_part.shape[1]
    half = r.mod_part.shape[2]
    seq_rows = r.hot[:, 0:seqs]
    grads = r.norm_wide[...]
    sums = [
        contract_rows(seq_rows, grads, HIGHEST),
        contract_rows(seq_rows, grads * r.normed[...], HIGHEST),
        contract_rows(r.hot[RIM : RIM + tokens, 0:seqs], r.branch[...], HIGHEST),
    ]
    whole = jnp.concatenate(sums, axis=1)
    r.mod_part[0] = whole[:, :half].astype(BF16)
    r.mod_part[1] = whole[:, half:].astype(BF16)


class ModSums:
    def __init__(self, place, r, sems):
        self.place, self.r, self.sems = place, r, sems
        self.core = place.bits[0]
        self.chip = place.bits[1] + 2 * place.bits[2]

    def copies(self, i):
        place, r, sems = self.place, self.r, self.sems
        if i == 0:
            return [remote(r.mod_part.at[1 - self.core], r.m1, sems, 0, place.flips[0])]
        if i == 1:
            peers = (place.flips[1], place.flips[2], place.flips[1] + place.flips[2] - place.me)
            return [
                remote(r.m1, r.m2.at[self.chip], sems, 1 + k, peer) for k, peer in enumerate(peers)
            ]
        if i == 2:
            return [
                remote(r.m1, r.m3.at[place.level], sems, 4 + k, g * PLANE + place.low)
                for k, g in enumerate(place.far)
            ]
        slot = 4 + len(place.far)
        return [
            remote(r.m4.at[self.core], r.m4.at[self.core], sems, slot, place.flips[0])
        ]

    def total(self, ref, number):
        total = ref[0].astype(F32)
        for g in range(1, number):
            total = total + ref[g].astype(F32)
        return total.astype(BF16)

    def step(self, i):
        place, r = self.place, self.r
        if i:
            for copy in self.copies(i - 1):
                copy.wait_recv()
        if i == 1:
            r.m1[...] = r.m1[...] + r.mod_part[self.core]
            r.m2[self.chip] = r.m1[...]
        elif i == 2:
            for copy in self.copies(1):
                copy.wait_send()
            summed = self.total(r.m2, 4)
            r.m1[...] = summed
            r.m3[place.level] = summed
        elif i == 3:
            r.m4[self.core] = self.total(r.m3, place.groups)
        for copy in self.copies(i):
            copy.start()

    def end(self, mod):
        half = mod.shape[1] // 2
        self.copies(3)[0].wait_recv()
        for c in range(2):
            mod[:, c * half : (c + 1) * half] = self.r.m4[c].astype(F32)[0 : mod.shape[0]]
        for i in (0, 2, 3):
            for copy in self.copies(i):
                copy.wait_send()


def late_columns(model, proj, rank, taps, states):
    first = proj + rank
    small = 2 * taps + 8 + 2 * states
    half = model // 2
    cut = half // 2 // LANES * LANES + LANES
    return 2 * (first + -first % LANES), half, cut, half - cut + small + -small % LANES


def block_kernel(count, names, lates, *refs):
    refs = list(refs)

    def take(size):
        taken = refs[:size]
        del refs[:size]
        return taken

    in_names, weight_names, out_names, scratch_names = names
    given = take(len(in_names))
    weights_any = take(5)
    outs = take(len(out_names))
    weights = take(len(weight_names))
    scratch = take(len(scratch_names))
    piece_refs = [take(6) for _ in range(8)]
    carry_sems = [take(2) for _ in range(3)]
    mod_sems, edge_sems, halo_sems = take(2), take(2), take(2)
    (load_sems,) = take(1)
    r = Refs(
        in_names + weight_names + out_names + scratch_names, given + weights + outs + scratch
    )
    tokens, inner = r.seed.shape
    blocks = inner // COLS
    scans = inner // SCAN
    r.decay_grad = (r.decay0, r.gate_branch)
    r.driven_grad = (r.driven0, r.gated_grad)

    w_mod_any, w_in_any, w_out_any, w_x_any, w_dt_any = weights_any
    model = r.hidden.shape[1]
    low_mod = r.kept.at[pl.ds(0, model), pl.ds(0, 2 * model)]
    high_mod = r.kept.at[pl.ds(model, model), pl.ds(0, model)]
    sources = (
        w_mod_any.at[:, pl.ds(0, 2 * model)],
        w_mod_any.at[:, pl.ds(2 * model, model)],
        w_in_any.at[:, pl.ds(0, inner)],
        w_in_any.at[:, pl.ds(inner, inner)],
        w_out_any,
        w_x_any,
        w_dt_any,
    )
    loads = [
        pltpu.make_async_copy(src, dst, load_sems.at[i])
        for i, (src, dst) in enumerate(zip(sources, [low_mod, high_mod] + weights))
    ]
    for load in loads:
        load.start()

    place = Place(count)
    barrier = pltpu.get_barrier_semaphore()
    peers = place.peers()
    for peer in peers:
        pl.semaphore_signal(barrier, inc=1, device_id=(peer,), device_id_type=MESH)
    me, core = place.me, place.bits[0]
    carries = Carries(r, place, carry_sems)
    views = (
        r.gate1.at[:, :, :, pl.ds(0, lates[0])],
        r.gate0,
        r.out0.at[:, :, :, pl.ds(0, lates[2])],
        r.out1.at[:, :, :, pl.ds(0, lates[3])],
    )
    parts = (r.gate0, r.gate1, r.out0, r.out1) + views
    pieces = [
        Piece(place, (XY, YX)[p % 2], part, part.at[core], piece_refs[p])
        for p, part in enumerate(parts)
    ]
    early, late = pieces[:4], pieces[4:]

    segment, wide_segment = token_masks(r, me * tokens)
    r.rate[...] = -jnp.exp(r.a_log[...]) * LOG2E
    r.out_acc[...] = jnp.zeros_like(r.out_acc)
    r.in_acc[...] = jnp.zeros_like(r.in_acc)
    r.small[...] = jnp.zeros_like(r.small)
    r.branch[...] = jnp.zeros_like(r.branch)
    r.norm_wide[...] = jnp.zeros_like(r.norm_wide)
    pl.semaphore_wait(barrier, len(peers))
    halos = [
        remote(r.hidden.at[pl.ds(tokens - 16, 16)], r.below, halo_sems, 0, place.right),
        remote(r.hidden.at[pl.ds(0, 16)], r.above, halo_sems, 1, place.left),
    ]
    for halo in halos:
        halo.start()
    cond = r.condition[...]
    cond_act = (cond * sigmoid(cond)).astype(BF16)
    loads[0].wait()
    loads[1].wait()
    seqs = cond.shape[0]
    r.modulation[0:seqs, 0 : 2 * model] = dot(cond_act, low_mod[...])
    r.modulation[0:seqs, 2 * model :] = dot(cond_act, high_mod[...])
    for halo in halos:
        halo.wait_recv()
    below = jnp.where(me > 0, r.below[...].astype(F32), 0.0)[16 - RIM :]
    above = jnp.where(me < count - 1, r.above[...].astype(F32), 0.0)[:RIM]
    normalise(r, below, above)
    modulate(r, segment, wide_segment)
    for load in loads[2:]:
        load.wait()
    project(r)
    coefficients(r, 0)
    stepping(r, 0)

    summarise(r, 0, 0, scans)
    carries.send(0)
    convolve_reverse(r)
    coefficients(r, 1)
    stepping(r, 1)
    carries.combine(0)
    summarise(r, 1, 0, scans - 1)
    carries.spread(0)
    summarise(r, 1, scans - 1, scans)
    carries.send(1)
    carries.receive(0)
    forward_scan(r, 0)
    carries.combine(1)
    adjoint_scan(r, 0, 0, scans - 1)
    carries.spread(1)
    adjoint_scan(r, 0, scans - 1, scans)
    carries.receive(1)
    forward_scan(r, 1)

    output_half(r, count, 0)
    early[0].step(0)
    output_half(r, count, 1)
    early[1].step(0)
    output_weights(r, count)
    early[2].step(0)
    early[3].step(0)
    r.output[...] = (r.hidden[...].astype(F32) + r.gate_rows[...] * r.branch[...]).astype(BF16)
    r.branch[...] = r.grad_out[...].astype(F32) * r.branch[...]
    early[0].step(1)
    early[1].step(1)
    adjoint_scan(r, 1, 0, 1)
    early[2].step(1)
    early[3].step(1)
    adjoint_scan(r, 1, 1, scans)
    through_steps(r)
    early[0].step(2)
    early[1].step(2)
    for piece in early:
        piece.release()
    fill_columns(r, views[0], count)
    late[0].step(0)
    through_conv(r, 0, blocks // 2)
    early[2].step(2)
    early[3].step(2)
    fill_conv(r, views[1:2], count)
    late[1].step(0)
    late[0].step(1)
    early[0].step(3)
    early[1].step(3)
    through_conv(r, blocks // 2, blocks)
    late[1].step(1)
    modulation_sums(r)
    mods = ModSums(place, r, mod_sems)
    mods.step(0)
    fill_conv(r, views[2:], count)
    late[2].step(0)
    late[3].step(0)
    mods.step(1)
    edges = [
        remote(
            r.norm_wide.at[pl.ds(0, RIM)],
            r.edge_got.at[pl.ds(RIM, RIM)],
            edge_sems,
            0,
            place.left,
        ),
        remote(
            r.norm_wide.at[pl.ds(r.norm_wide.shape[0] - RIM, RIM)],
            r.edge_got.at[pl.ds(0, RIM)],
            edge_sems,
            1,
            place.right,
        ),
    ]
    for copy in edges:
        copy.start()
    late[2].step(1)
    late[3].step(1)
    early[2].step(3)
    early[3].step(3)
    late[0].step(2)
    late[1].step(2)
    mods.step(2)
    width = r.share_early.shape[1] // 4
    for p, at in enumerate((2, 3, 0, 1)):
        early[p].end(r.share_early, at * width)
    late[2].step(2)
    late[3].step(2)
    late[0].step(3)
    late[1].step(3)
    mods.step(3)
    for copy in edges:
        copy.wait_recv()
    input_gradient(r, place)
    late[2].step(3)
    late[3].step(3)
    mods.end(r.mod)
    modulation_shares(r, place)
    begin = 0
    for piece, view in zip(late, views):
        piece.end(r.share_late, begin)
        piece.release()
        begin += view.shape[3]
    carries.finish()
    for copy in edges + halos:
        copy.wait_send()


def run_block(count, given, weights):
    w_mod, w_in, w_out, w_x, w_dt = weights
    tokens, model = given.hidden.shape
    inner = w_in.shape[1] // 2
    rank = w_dt.shape[1]
    proj = w_x.shape[1]
    states = given.a_log.shape[1]
    taps = given.conv_w.shape[1]
    groups = count // PLANE
    wide = tokens + 2 * RIM
    tiles = inner // LANES
    share = 2 * tiles // PLANE
    rows = slot_rows(count, inner)
    lates = late_columns(model, proj, rank, taps, states)
    small = lates[3] - (model // 2 - lates[2])
    both = (2, tokens, inner)
    spread = (2, tokens * states, LANES)
    diag = (2, tokens, CHUNK * states)
    mod = (8, 3 * model)
    half_mod = (16, 3 * model // 2)
    slots = pltpu.VMEM((2, count // 2, rows, model // 2), BF16)
    buffer = pltpu.VMEM((CHUNK * states, SCAN), BF16)
    full = pltpu.VMEM((tokens, inner), F32)
    outs = dict(
        output=shaped((tokens, model), BF16),
        grad_x=shaped((tokens, model)),
        w_mod_share=shaped((model // count, 3 * model)),
        b_mod_share=shaped((1, 3 * model // count)),
        share_early=shaped((rows, 2 * model)),
        share_late=shaped((rows, sum(lates))),
    )
    held = dict(
        w_conv=pltpu.VMEM((model, inner), BF16),
        w_gate=pltpu.VMEM((model, inner), BF16),
        w_out=pltpu.VMEM(w_out.shape, BF16),
        w_x=pltpu.VMEM(w_x.shape, BF16),
        w_dt=pltpu.VMEM(w_dt.shape, BF16),
    )
    scratch = dict(
        mixer=pltpu.VMEM((wide, model), BF16),
        mixer_own=pltpu.VMEM((tokens, model), BF16),
        normed=pltpu.VMEM((wide, model), F32),
        rescale=pltpu.VMEM((tokens, LANES), F32),
        scale1=pltpu.VMEM((tokens, model), F32),
        gate_rows=pltpu.VMEM((tokens, model), F32),
        branch_grad=pltpu.VMEM((tokens, model), BF16),
        conv_keep=pltpu.VMEM((wide, inner), BF16),
        conv_wide=pltpu.VMEM((wide, COLS), F32),
        conv_slope=pltpu.VMEM(both, BF16),
        active=pltpu.VMEM(both, BF16),
        gate_branch=full,
        gated_grad=full,
        seed=full,
        proj=pltpu.VMEM((2, tokens, proj), F32),
        rank_low=pltpu.VMEM((2, tokens, rank), BF16),
        masked=pltpu.VMEM(both, F32),
        driven=pltpu.VMEM(both, F32),
        in_spread=pltpu.VMEM(spread, F32),
        out_spread=pltpu.VMEM(spread, F32),
        in_blk=pltpu.VMEM(diag, BF16),
        out_blk=pltpu.VMEM(diag, BF16),
        rate=pltpu.VMEM((2, states, inner), F32),
        masks=pltpu.VMEM((2 * taps - 1, tokens, LANES), F32),
        hot=pltpu.VMEM((wide, LANES), F32),
        below=pltpu.VMEM((16, model), BF16),
        above=pltpu.VMEM((16, model), BF16),
        modulation=pltpu.VMEM((8, w_mod.shape[1]), F32),
        sums=pltpu.VMEM((2 * tiles, 3, states, LANES), BF16),
        got=pltpu.VMEM((PLANE, share, 3, states, LANES), BF16),
        total=pltpu.VMEM((3, share, states, LANES), BF16),
        others=pltpu.VMEM((groups, 2, share, states, LANES), BF16),
        back=pltpu.VMEM((PLANE, share, 2, states, LANES), BF16),
        entering=pltpu.VMEM((2 * tiles, 2, states, LANES), BF16),
        kept=pltpu.VMEM(((tokens + 1) * states, inner), BF16),
        rows0=buffer,
        rows1=buffer,
        slope0=buffer,
        slope1=buffer,
        mixed=full,
        decay0=full,
        driven0=full,
        out_acc=pltpu.VMEM(diag, F32),
        in_acc=pltpu.VMEM(diag, F32),
        gated=pltpu.VMEM((tokens, inner), BF16),
        gate_branch_grad=pltpu.VMEM((tokens, inner), BF16),
        branch=pltpu.VMEM((tokens, model), F32),
        whole=pltpu.VMEM((model, inner // 2), F32),
        stage=pltpu.VMEM((rows, model // 2), F32),
        gate0=slots,
        gate1=slots,
        out0=slots,
        out1=slots,
        small=pltpu.VMEM((small, inner), F32),
        rank_grad=pltpu.VMEM((2, tokens, rank), F32),
        proj_grad=pltpu.VMEM((2, tokens, proj), BF16),
        input_wide=pltpu.VMEM((wide, COLS), F32),
        small_cols=pltpu.VMEM((inner, small), F32),
        norm_wide=pltpu.VMEM((wide, model), F32),
        mod_part=pltpu.VMEM((2,) + half_mod, BF16),
        m1=pltpu.VMEM(half_mod, BF16),
        m2=pltpu.VMEM((4,) + half_mod, BF16),
        m3=pltpu.VMEM((groups,) + half_mod, BF16),
        m4=pltpu.VMEM((2,) + half_mod, BF16),
        mod=pltpu.VMEM(mod, F32),
        edge_got=pltpu.VMEM((2 * RIM, model), F32),
    )
    sems = pltpu.SemaphoreType.DMA
    pieces = []
    for cols in (model // 2,) * 4 + lates:
        pieces += piece_scratch(rows, cols, groups)
    given = vars(given)
    names = tuple(tuple(part) for part in (given, held, outs, scratch))
    return pl.pallas_call(
        functools.partial(block_kernel, count, names, lates),
        in_specs=[pl.BlockSpec(memory_space=pltpu.SMEM)] + [VMEM] * (len(given) - 1) + [ANY] * 5,
        out_specs=[VMEM] * len(outs),
        out_shape=list(outs.values()),
        scratch_shapes=list(held.values())
        + list(scratch.values())
        + pieces
        + [sems((PLANE,))] * 2
        + [sems((groups,))] * 2
        + [sems((PLANE,))] * 2
        + [sems((6 + groups,))] * 2
        + [sems((2,))] * 4
        + [sems((len(held) + 2,))],
        compiler_params=pltpu.CompilerParams(
            collective_id=0, has_side_effects=True, vmem_limit_bytes=63 * MIB
        ),
        name="block",
    )(*given.values(), *weights)


def finish_kernel(
    count,
    proj,
    rank,
    taps,
    states,
    share_early,
    share_late,
    made,
    made_grad,
    made_w_mod,
    made_b_mod,
    output,
    grad_x,
    w_mod,
    b_mod,
    w_in,
    conv_w,
    conv_b,
    w_x,
    w_dt,
    dt_bias,
    a_log,
    d_skip,
    w_out,
):
    tokens, model = output.shape
    mrows, double = w_in.shape
    inner = double // 2
    rows = w_out.shape[0]
    half = model // 2
    first = late_columns(model, proj, rank, taps, states)[0]

    output[...] = made[...]
    grad_x[...] = made_grad[...]
    w_mod[...] = made_w_mod[...]
    b_mod[...] = made_b_mod[...]
    w_out[...] = share_early[0:rows, 0:model]
    for i in range(2):
        low = share_late[:, first + i * half : first + (i + 1) * half]
        high = share_early[:, model + i * half : model + (i + 1) * half]
        for at, both in ((i * model, low), (inner + i * model, high)):
            w_in[:, at : at + half] = both[0:mrows]
            w_in[:, at + half : at + model] = both[mrows : 2 * mrows]

    flipped = share_late[:, 0:first].T
    for d in range(2):
        at = d * first // 2
        w_x[d] = share_late[0:rows, at : at + proj]
        w_dt[d] = flipped[at + proj : at + proj + rank, 0:rows]
    flipped = share_late[:, first + model :].T
    for d in range(2):
        conv_w[d] = flipped[d * taps : (d + 1) * taps, 0:rows]
    at = 2 * taps
    conv_b[...] = flipped[at : at + 2, 0:rows]
    dt_bias[...] = flipped[at + 2 : at + 4, 0:rows]
    d_skip[...] = flipped[at + 4 : at + 6, 0:rows]
    at = at + 8
    for d in range(2):
        a_log[d] = flipped[at + d * states : at + (d + 1) * states, 0:rows]


def on_device(
    count,
    hidden,
    condition,
    seq_lengths,
    w_mod,
    b_mod,
    w_in,
    conv_w,
    conv_b,
    w_x,
    w_dt,
    dt_bias,
    a_log,
    d_skip,
    w_out,
    grad_out,
):
    tokens, model = hidden.shape
    inner = w_in.shape[1] // 2
    rank = w_dt.shape[1]
    proj = w_x.shape[2]
    states = a_log.shape[1]
    taps = conv_w.shape[1]
    rows, mrows = inner // count, model // count
    given = types.SimpleNamespace(
        lengths=seq_lengths,
        hidden=hidden,
        condition=condition,
        b_mod=b_mod.reshape(-1, LANES),
        conv_w=conv_w,
        conv_b=conv_b,
        dt_bias=dt_bias,
        d_skip=d_skip,
        a_log=a_log,
        grad_out=grad_out,
    )
    weights = (w_mod, w_in, w_out, jnp.swapaxes(w_x, 1, 2), w_dt)
    output, grad_x, w_mod_share, b_mod_share, share_early, share_late = run_block(
        count, given, weights
    )
    results = pl.pallas_call(
        functools.partial(finish_kernel, count, proj, rank, taps, states),
        in_specs=[VMEM] * 6,
        out_specs=[VMEM] * 13,
        out_shape=[
            shaped((tokens, model), BF16),
            shaped((tokens, model)),
            shaped((mrows, 3 * model)),
            shaped((1, 3 * model // count)),
            shaped((mrows, 2 * inner)),
            shaped((2, taps, rows)),
            shaped((2, rows)),
            shaped((2, rows, proj)),
            shaped((2, rank, rows)),
            shaped((2, rows)),
            shaped((2, states, rows)),
            shaped((2, rows)),
            shaped((rows, model)),
        ],
        compiler_params=pltpu.CompilerParams(vmem_limit_bytes=60 * MIB),
        name="finish",
    )(share_early, share_late, output, grad_x, w_mod_share, b_mod_share)
    return tuple(results[:3]) + (results[3].reshape(-1),) + tuple(results[4:])


def solution(mesh):
    in_specs = (P("seq", None),) + (P(),) * 13 + (P("seq", None),)
    out_specs = (
        P("seq", None),
        P("seq", None),
        P("seq", None),
        P("seq"),
        P("seq", None),
        P(None, None, "seq"),
        P(None, "seq"),
        P(None, "seq", None),
        P(None, None, "seq"),
        P(None, "seq"),
        P(None, None, "seq"),
        P(None, "seq"),
        P("seq", None),
    )
    return jax.shard_map(
        functools.partial(on_device, mesh.shape["seq"]),
        mesh=mesh,
        in_specs=in_specs,
        out_specs=out_specs,
        check_vma=False,
    )
```

profile of v0, /device:TPU:0, one launch (start us, length us, event | category | flops | bytes accessed | tf_op | source)
XLA Modules:
  0.0 114.2 jit_solution(15354385726815794975)
XLA Ops:
  0.7 111.0 %block.1 = (bf16[128,768]{1,0:T(8,128)(2,1)}, f32[128,768]{1,0:T(8,128)}, f32[24,2304]{1,0:T(8,128)}, f32[1,72]{1,0:T(1,128)}, f32[48,1536]{1,0:T(8,128)}, /*index=5*/f32[48,1152]{1,0:T(8,128)}) custom-call(s32[6]{0:T(128)} %refs_0_.1, bf16[128,768]{1,0:T(8,128)(2,1)} %refs_1_.1, f32[6,768]{1,0:T(8,128)} %refs_2_.1, f32[18,128]{1,0:T(8,128)} %bitcast.4, ...), custom_call_target="tpu_custom_call" | custom-call | tf_op jit(solution)/shard_map/block/pallas_call | solution.py:1369
  111.7 2.4 %finish.1 = (bf16[128,768]{1,0:T(8,128)(2,1)}, f32[128,768]{1,0:T(8,128)}, f32[24,2304]{1,0:T(8,128)}, f32[1,72]{1,0:T(1,128)}, f32[24,3072]{1,0:T(8,128)}, /*in...) custom-call(f32[48,1536]{1,0:T(8,128)} %get-tuple-element.32.share_e, ...), custom_call_target="tpu_custom_call" | custom-call | tf_op jit(solution)/shard_map/finish/pallas_call | solution.py:1493
where the time goes:
time: 114 us
  Pallas kernels  113 us (99%)
    pallas_call x1, Pallas kernels, run_block(): pl.pallas_call(functools.partial(block_kernel, count, names, lates), in_s...  111 us
    pallas_call x1, Pallas kernels, on_device(): pl.pallas_call(functools.partial(finish_kernel, count, proj, rank, taps,...  2.43 us

commit v1 on v0

--- a/solution.py
+++ b/solution.py
@@ -191,10 +191,10 @@
         total = jnp.broadcast_to(r.conv_b[d : d + 1, lanes], (tokens, LANES))
         for k in range(taps):
             offset = offset_of(d, k, taps)
-            total = total + r.conv_w[d, k : k + 1, lanes] * (
-                r.conv_wide[RIM + offset : RIM + offset + tokens, here]
-                * r.masks[offset + taps - 1]
-            )
+            tap = r.conv_wide[RIM + offset : RIM + offset + tokens, here]
+            if offset:
+                tap = tap * r.masks[offset + taps - 1]
+            total = total + r.conv_w[d, k : k + 1, lanes] * tap
         sigma = sigmoid(total)
         r.conv_slope[d, :, lanes] = (sigma * (1.0 + total * (1.0 - sigma))).astype(BF16)
         act = (total * sigma).astype(BF16)
@@ -879,7 +879,7 @@
                 for k in range(taps):
                     offset = offset_of(d, k, taps)
                     window = slice(RIM + offset, RIM + offset + tokens)
-                    part = grad * r.masks[offset + taps - 1]
+                    part = grad * r.masks[offset + taps - 1] if offset else grad
                     at = at_conv + d * taps + k
                     r.small[at : at + 1, lanes] = column_sum(part * r.conv_wide[window, here])
                     r.input_wide[window, here] += r.conv_w[d, k : k + 1, lanes] * part
@@ -938,11 +938,11 @@
 
     cond = r.condition[...]
     cond_act = (cond * sigmoid(cond)).astype(BF16)
-    my_cond = dot(cond_act, picked(model, mrows).astype(BF16))
-    totals = r.mod[0:seqs, :]
-    r.w_mod_share[...] = contract_rows(my_cond, totals, HIGHEST)
-    bias = jnp.broadcast_to(jnp.sum(totals, axis=0, keepdims=True), (8, 3 * model))
-    r.b_mod_share[...] = dot(bias, picked(3 * model, width).astype(F32), precision=HIGHEST)[0:1]
+    my_cond = dot(cond_act, picked(model, mrows).astype(BF16)).astype(BF16)
+    totals = r.mod[...].astype(BF16)
+    r.w_mod_share[...] = contract_rows(my_cond, totals[0:seqs])
+    mine = dot(totals, picked(3 * model, width).astype(BF16))
+    r.b_mod_share[...] = jnp.sum(mine[0:seqs], axis=0, keepdims=True)
 
 
 def input_gradient(r, place):
@@ -1203,6 +1203,8 @@
     fill_conv(r, views[2:], count)
     late[2].step(0)
     late[3].step(0)
+    late[2].step(1)
+    late[3].step(1)
     mods.step(1)
     edges = [
         remote(
@@ -1222,16 +1224,11 @@
     ]
     for copy in edges:
         copy.start()
-    late[2].step(1)
-    late[3].step(1)
     early[2].step(3)
     early[3].step(3)
     late[0].step(2)
     late[1].step(2)
     mods.step(2)
-    width = r.share_early.shape[1] // 4
-    for p, at in enumerate((2, 3, 0, 1)):
-        early[p].end(r.share_early, at * width)
     late[2].step(2)
     late[3].step(2)
     late[0].step(3)
@@ -1242,6 +1239,9 @@
     input_gradient(r, place)
     late[2].step(3)
     late[3].step(3)
+    width = r.share_early.shape[1] // 4
+    for p, at in enumerate((2, 3, 0, 1)):
+        early[p].end(r.share_early, at * width)
     mods.end(r.mod)
     modulation_shares(r, place)
     begin = 0

time: 114 us -> 116 us (1.018)
  Pallas kernels: 113 us -> 115 us
    pallas_call x1, Pallas kernels: 111 us -> 113 us  [run_block(): pl.pallas_call(functools.partial(block_kernel, count, names, lates), in_s...]
where the time goes in v1:
time: 116 us
  Pallas kernels  115 us (99%)
    pallas_call x1, Pallas kernels, run_block(): pl.pallas_call(functools.partial(block_kernel, count, names, lates), in_s...  113 us
    pallas_call x1, Pallas kernels, on_device(): pl.pallas_call(functools.partial(finish_kernel, count, proj, rank, taps,...  2.43 us

profile of v1, /device:TPU:0, one launch (start us, length us, event | category | flops | bytes accessed | tf_op | source)
XLA Modules:
  0.0 115.8 jit_solution(18132191171630664307)
XLA Ops:
  0.7 112.6 %block.1 = (bf16[128,768]{1,0:T(8,128)(2,1)}, f32[128,768]{1,0:T(8,128)}, f32[24,2304]{1,0:T(8,128)}, f32[1,72]{1,0:T(1,128)}, f32[48,1536]{1,0:T(8,128)}, /*index=5*/f32[48,1152]{1,0:T(8,128)}) custom-call(s32[6]{0:T(128)} %refs_0_.1, bf16[128,768]{1,0:T(8,128)(2,1)} %refs_1_.1, f32[6,768]{1,0:T(8,128)} %refs_2_.1, f32[18,128]{1,0:T(8,128)} %bitcast.4, ...), custom_call_target="tpu_custom_call" | custom-call | tf_op jit(solution)/shard_map/block/pallas_call | solution.py:1369
  113.3 2.4 %finish.1 = (bf16[128,768]{1,0:T(8,128)(2,1)}, f32[128,768]{1,0:T(8,128)}, f32[24,2304]{1,0:T(8,128)}, f32[1,72]{1,0:T(1,128)}, f32[24,3072]{1,0:T(8,128)}, /*in...) custom-call(f32[48,1536]{1,0:T(8,128)} %get-tuple-element.32.share_e, ...), custom_call_target="tpu_custom_call" | custom-call | tf_op jit(solution)/shard_map/finish/pallas_call | solution.py:1493
